TPU v7x, 32 devices: a whole 2x2x4 slice. The times are simulated.
32 devices in a mesh: replica: 8 (over y, x, core), fsdp: 4 (over z).
Axes of the slice: x: 2, y: 2, z: 4, core: 2. Of those that a mesh axis runs over, the one named last changes fastest.
Arguments:
- activations: bfloat16 [8, 1792, 4096], P('replica', 'fsdp'), may hold values from -84 to 84
- targets: bfloat16 [8, 1792, 512], P('replica', 'fsdp'), may hold values from -8 to 8
- weights: float32 [8, 4096, 512], P('replica', 'fsdp'), may hold values from -19 to 19
- lengths: int32 [8, 28], P('replica'), may hold values from 1 to 64, 896 in all within a row
Outputs:
- averaged: float32 [8, 4096, 512], P('replica', 'fsdp')
Inputs may be any that keep to these rules, and one draw needn't show every extreme that they name: `lengths`: each row sums to 896; sequence s of a replica fills slot s from its first position.
All inputs are finite; a program needn't handle non-finite values.
Results may differ from a plain program's by a relative error of at most 0.0014.
Values may be sent and summed in bfloat16 or wider, within the bound.
No kernel may reach another device: no remote copies, remote signals or barrier semaphores. Data moves between devices by JAX's collectives and lax.ppermute only.
A program may use at most 64 MiB of HBM per device.

v0:
```python
import jax
import jax.numpy as jnp
from jax import lax
from jax.sharding import PartitionSpec as P

SLOT = 64
STEP = 3


learning_rate = 0.1
epsilon = 1e-06


def swapped(value, axis, bit):
    mask = 2**bit
    pairs = [(source, source ^ mask) for source in range(lax.axis_size(axis))]
    return lax.ppermute(value, axis, pairs)


def local(activations, targets, weights, lengths):
    features = activations[0]
    wanted = targets[0]
    master = weights[0]
    lengths_row = lengths[0]
    tokens_here = features.shape[0]
    local_rows = master.shape[0]
    columns = master.shape[1]
    members = lax.axis_size("fsdp")
    distance_bit = STEP % (lax.axis_size("replica").bit_length() - 1)
    feature_block = features
    projected = jnp.dot(
        feature_block,
        lax.all_gather(master.astype(jnp.bfloat16), "fsdp", axis=0, tiled=True),
        preferred_element_type=jnp.float32,
    )
    keys_out = projected * features.shape[1] ** (-0.5)
    sequences_here = tokens_here // SLOT
    first_sequence = lax.axis_index("fsdp") * sequences_here
    local_lengths = lax.dynamic_slice_in_dim(lengths_row, first_sequence, sequences_here)
    slot_positions = jnp.arange(SLOT, dtype=jnp.int32)
    live_mask = (slot_positions[None, :] < local_lengths[:, None]).reshape(tokens_here)
    residual = jnp.where(live_mask[:, None], keys_out - wanted.astype(jnp.float32), 0.0).astype(
        jnp.bfloat16
    )
    feature_block = features
    gradient = lax.psum_scatter(
        lax.dot_general(
            feature_block, residual, (((0,), (0,)), ((), ())), preferred_element_type=jnp.float32
        ).astype(jnp.bfloat16),
        "fsdp",
        scatter_dimension=0,
        tiled=True,
    ).astype(jnp.float32)
    square_sum = lax.psum(jnp.sum(gradient * gradient), "fsdp")
    entries = members * local_rows * columns
    direction = gradient * lax.rsqrt(square_sum / entries + epsilon)
    updated = master - learning_rate * direction
    partner_updated = swapped(updated, "replica", distance_bit)
    averaged = 0.5 * (updated + partner_updated)
    return averaged[None]


def solution(mesh):
    return jax.shard_map(
        local,
        mesh=mesh,
        in_specs=(
            P("replica", "fsdp", None),
            P("replica", "fsdp", None),
            P("replica", "fsdp", None),
            P("replica", None),
        ),
        out_specs=P("replica", "fsdp", None),
        check_vma=False,
    )
```

profile of v0, /device:TPU:7, one launch (start us, length us, event | category | flops | bytes accessed | tf_op | source)
XLA Modules:
  0.0 208.0 jit_solution(151454939389940601)
XLA Ops:
  6.5 0.0 copy-start
  6.5 0.0 all-gather.2.cloned.1.call-start
  6.5 1.9 copy.5
  8.5 0.0 copy-start.1
  8.5 1.1 bitcast_convert_fusion
  9.6 0.0 all-gather.2.cloned.1.call-update
  9.6 0.0 reduce-scatter.2.cloned.1.call-start
  9.7 0.0 copy-done
  9.7 0.1 dynamic-slice_bitcast_fusion
  9.8 0.1 iota_compare_fusion
  9.9 0.1 lt.30
  10.0 81.8 %all-gather.2.cloned.1.call-done = bf16[4096,512]{0,1:T(8,128)(2,1)} async-done(((bf16[1024,512]{0,1:T(8,128)(2,1)}), bf16[4096,512]{0,1:T(8,128)(2,1)}) %all-gather.2.cloned.1.call-update) | async-done | bytes 4194320 | tf_op jit(solution)/shard_map/all_gather | solution.py:33
  91.8 0.0 copy-done.1
  91.8 10.7 %fusion = bf16[4096,512]{0,1:T(8,128)(2,1)} fusion(bf16[1,448,4096]{2,1,0:T(8,128)(2,1)} %param.4, bf16[4096,512]{0,1:T(8,128)(2,1)} %all-gather.2.cloned.1.call-done, bf16[1,448,512]{2,1,0:T(8,128)(2,1)S(1)} %copy-done.1, pred[448]{0:T(512)(128)(4,1)S(1)} %lt.30), kind=kOutput, calls=%fused_computation.1 | convolution fusion | flops 3761340416 | bytes 12517824 | tf_op jit(solution)/shard_map/dot_general | solution.py:47
  102.5 0.0 reduce-scatter.2.cloned.1.call-update
  102.5 75.5 %reduce-scatter.2.cloned.1.call-done = bf16[1024,512]{0,1:T(8,128)(2,1)} async-done(((bf16[4096,512]{0,1:T(8,128)(2,1)}), bf16[1024,512]{0,1:T(8,128)(2,1)}) %reduce-scatter.2.cloned.1.call-update) | async-done | bytes 1048592 | tf_op jit(solution)/shard_map/reduce_scatter | solution.py:46
  178.0 2.4 %fusion.4 = f32[]{:T(128)} fusion(bf16[1024,512]{0,1:T(8,128)(2,1)} %reduce-scatter.2.cloned.1.call-done), kind=kLoop, calls=%fused_computation.7 | loop fusion | flops 1572863 | bytes 1048580 | tf_op jit(solution)/shard_map/reduce_sum | solution.py:54
  180.3 9.8 %psum.7 = f32[]{:T(128)} all-reduce(f32[]{:T(128)} %fusion.4), channel_id=1, replica_groups=mesh['replica'=8,'fsdp'=4] {'fsdp'}, use_global_device_ids=true, to_apply=%region_2.3 | all-reduce | flops 1 | bytes 8 | tf_op jit(solution)/shard_map/psum | solution.py:54
  190.8 1.6 fusion.6
  192.4 2.7 %collective-permute-start = (f32[1024,512]{0,1:T(8,128)S(1)}, f32[1024,512]{0,1:T(8,128)S(1)}, u32[]{:S(2)}, u32[]{:S(2)}) collective-permute-start(f32[1024,512]{0,1:T(8,128)S(1)} %fusion.6), channel_id=1, source_target_pairs={{0,4},{4,0},{8,12},{12,8},{16,20},{20,16},{24,28},{28,24},{1,5},{5... | collective-permute-start | bytes 6291464 | tf_op jit(solution)/shard_map/ppermute | solution.py:17
  195.2 3.8 %collective-permute-done = f32[1024,512]{0,1:T(8,128)S(1)} collective-permute-done((f32[1024,512]{0,1:T(8,128)S(1)}, f32[1024,512]{0,1:T(8,128)S(1)}, u32[]{:S(2)}, u32[]{:S(2)}) %collective-permute-start) | collective-permute-done | bytes 2097184 | tf_op jit(solution)/shard_map/ppermute | solution.py:17
  198.9 0.4 multiply_bitcast_fusion
  199.4 1.8 copy.6
Async XLA Ops:
  6.5 3.2 %copy-start = (s32[1,28]{1,0:T(1,128)S(1)}, s32[1,28]{1,0:T(1,128)}, u32[]{:S(2)}) copy-start(s32[1,28]{1,0:T(1,128)} %param.7) | copy-start | bytes 340
  6.5 85.2 %all-gather.2.cloned.1.call-start = ((), (), s32[]{:S(2)}) async-start(), calls=%async_computation.1 | async-start | bytes 5242880 | tf_op jit(solution)/shard_map/all_gather | solution.py:33
  8.5 83.3 %copy-start.1 = (bf16[1,448,512]{2,1,0:T(8,128)(2,1)S(1)}, bf16[1,448,512]{2,1,0:T(8,128)(2,1)}, u32[]{:S(2)}) copy-start(bf16[1,448,512]{2,1,0:T(8,128)(2,1)} %param.5) | copy-start | bytes 1376260
  9.6 168.3 %reduce-scatter.2.cloned.1.call-start = ((), (), s32[]{:S(2)}) async-start(), calls=%async_computation.2 | async-start | bytes 5242880 | tf_op jit(solution)/shard_map/reduce_scatter | solution.py:46
  192.4 6.5 %collective-permute-start = (f32[1024,512]{0,1:T(8,128)S(1)}, f32[1024,512]{0,1:T(8,128)S(1)}, u32[]{:S(2)}, u32[]{:S(2)}) collective-permute-start(f32[1024,512]{0,1:T(8,128)S(1)} %fusion.6), channel_id=1, source_target_pairs={{0,4},{4,0},{8,12},{12,8},{16,20},{20,16},{24,28},{28,24},{1,5},{5... | collective-permute-start | bytes 6291464 | tf_op jit(solution)/shard_map/ppermute | solution.py:17
Sparse Core Ops, SparseCore 0:
  9.8 81.9 all-gather.1
  102.6 75.2 reduce-scatter.1
where the time goes:
time: 209 us; the launch traced here: 208 us
  waiting for transfers between devices  161 us (77%)
  between operations  14.1 us (7%)
  matrix products  10.7 us (5%)
  blocking collectives  9.78 us (5%)
  other arithmetic  5.61 us (3%)
  local copies, waits for them, and re-layouts  3.92 us (2%)
  starting transfers between devices  2.76 us (1%)
    all_gather x1, waiting for transfers between devices, local(): lax.all_gather(master.astype(jnp.bfloat16), 'fsdp', axis=0, tiled=True)  81.8 us
    reduce_scatter x1, waiting for transfers between devices, local(): lax.psum_scatter(lax.dot_general(feature_block, residual, (((0,), (0,)),...  75.5 us
    dot_general x1, matrix products, local(): lax.dot_general(feature_block, residual, (((0,), (0,)), ((), ())), prefer...  10.7 us
    psum x1, blocking collectives, local(): square_sum = lax.psum(jnp.sum(gradient * gradient), 'fsdp')  9.78 us
  transfers between devices with their start and end apart: 3, of which 3 were waited for; matrix products, arithmetic and copies ran while one was open for 0% of the time, Pallas kernels for 0%

commit v1 on v0

v1 whole, which is shorter than its diff:
```python
import jax
import jax.numpy as jnp
from jax import lax
from jax.sharding import PartitionSpec as P

SLOT = 64
STEP = 3
PARTS = 4

learning_rate = 0.1
epsilon = 1e-06


def swapped(value, axis, bit):
    mask = 2**bit
    pairs = [(source, source ^ mask) for source in range(lax.axis_size(axis))]
    return lax.ppermute(value, axis, pairs)


def moved(value, senders, distance):
    return lax.ppermute(value, "fsdp", [(source, source + distance) for source in senders])


def gathered(own, members, index):
    rights, lefts = [own], [own]
    for i in range(1, members):
        rights.append(moved(rights[-1], range(i - 1, members - 1), 1))
        lefts.append(moved(lefts[-1], range(1, members - i + 1), -1))
    return [own] + [
        jnp.where(index >= i, rights[i], lefts[members - i]) for i in range(1, members)
    ]


def reduced(terms, members):
    def added(received, term):
        return (received.astype(jnp.float32) + term.astype(jnp.float32)).astype(term.dtype)

    right, left = terms[members - 1], terms[1]
    for i in range(1, members):
        right = moved(right, range(0, i), 1)
        left = moved(left, range(members - i, members), -1)
        if i < members - 1:
            right = added(right, terms[members - i - 1])
            left = added(left, terms[i + 1])
    return terms[0].astype(jnp.float32) + right.astype(jnp.float32) + left.astype(jnp.float32)


def local(activations, targets, weights, lengths):
    features = activations[0]
    wanted = targets[0]
    master = weights[0]
    lengths_row = lengths[0]
    tokens_here = features.shape[0]
    local_rows, columns = master.shape
    members = lax.axis_size("fsdp")
    index = lax.axis_index("fsdp")
    distance_bit = STEP % (lax.axis_size("replica").bit_length() - 1)
    width = columns // PARTS

    sequences_here = tokens_here // SLOT
    local_lengths = lax.dynamic_slice_in_dim(lengths_row, index * sequences_here, sequences_here)
    slot_positions = jnp.arange(SLOT, dtype=jnp.int32)
    live = (slot_positions[None, :] < local_lengths[:, None]).reshape(tokens_here)[:, None]

    blocks = [
        lax.dynamic_slice_in_dim(features, ((index + i) % members) * local_rows, local_rows, axis=1)
        for i in range(members)
    ]
    low = master.astype(jnp.bfloat16)
    halves = 0.5 * (master + swapped(master, "replica", distance_bit))

    gradients, partners = [], []
    for part in range(PARTS):
        cut = slice(part * width, (part + 1) * width)
        weight_blocks = gathered(low[:, cut], members, index)
        projected = sum(
            jnp.dot(
                blocks[(members - i) % members],
                weight_blocks[i],
                preferred_element_type=jnp.float32,
            )
            for i in range(members)
        )
        keys_out = projected * features.shape[1] ** (-0.5)
        residual = jnp.where(live, keys_out - wanted[:, cut].astype(jnp.float32), 0.0).astype(
            jnp.bfloat16
        )
        terms = [
            lax.dot_general(
                block, residual, (((0,), (0,)), ((), ())), preferred_element_type=jnp.float32
            ).astype(jnp.bfloat16)
            for block in blocks
        ]
        gradient = reduced(terms, members)
        gradients.append(gradient)
        partners.append(swapped(gradient, "replica", distance_bit))

    squares = jnp.stack(
        [sum(jnp.sum(g * g) for g in gradients), sum(jnp.sum(g * g) for g in partners)]
    )
    total = squares
    for i in range(1, members):
        ring = [(source, (source + i) % members) for source in range(members)]
        total = total + lax.ppermute(squares, "fsdp", ring)
    scales = lax.rsqrt(total / (members * local_rows * columns) + epsilon)
    step = 0.5 * learning_rate
    averaged = [
        halves[:, part * width : (part + 1) * width]
        - step * (gradients[part] * scales[0] + partners[part] * scales[1])
        for part in range(PARTS)
    ]
    return jnp.concatenate(averaged, axis=1)[None]


def solution(mesh):
    return jax.shard_map(
        local,
        mesh=mesh,
        in_specs=(
            P("replica", "fsdp", None),
            P("replica", "fsdp", None),
            P("replica", "fsdp", None),
            P("replica", None),
        ),
        out_specs=P("replica", "fsdp", None),
        check_vma=False,
    )
```

time: 209 us -> 201 us (0.962); the launches traced: 208 us -> 197 us
  waiting for transfers between devices: 161 us -> 23.2 us
  starting transfers between devices: 2.76 us -> 120 us
  other arithmetic: 5.61 us -> 18.9 us
  matrix products: 10.7 us -> 23.1 us
  blocking collectives: 9.78 us -> 0 us
  between operations: 14.1 us -> 6.12 us
    ppermute x0 -> x51, starting transfers between devices: none -> 101 us  [the longest x48 96 us: moved(): lax.ppermute(value, 'fsdp', [(source, source + distance) for source in se...]
    all_gather x1 -> x0, waiting for transfers between devices: 81.8 us -> none  [local(): lax.all_gather(master.astype(jnp.bfloat16), 'fsdp', axis=0, tiled=True)]
    reduce_scatter x1 -> x0, waiting for transfers between devices: 75.5 us -> none  [local(): lax.psum_scatter(lax.dot_general(feature_block, residual, (((0,), (0,)),...]
    ppermute x0 -> x51, waiting for transfers between devices: none -> 23.1 us  [the longest x48 21.8 us: moved(): lax.ppermute(value, 'fsdp', [(source, source + distance) for source in se...]
    ppermute x1 -> x5, starting transfers between devices: 2.72 us -> 19.4 us  [swapped(): return lax.ppermute(value, axis, pairs)]
    dot_general x1 -> x32, matrix products: 10.7 us -> 23.1 us  [the longest x16 17.4 us: local(): jnp.dot(blocks[(members - i) % members], weight_blocks[i], preferred_elem...]
    psum x1 -> x0, blocking collectives: 9.78 us -> none  [local(): square_sum = lax.psum(jnp.sum(gradient * gradient), 'fsdp')]
    reduce_sum x1 -> x8, other arithmetic: 2.37 us -> 11.9 us  [local(): jnp.sum(g * g)]
  transfers between devices with their start and end apart: 3 -> 56, of which waited for: 3 -> 12; matrix products, arithmetic and copies ran while one was open for 0% -> 19% of each run, Pallas kernels for 0% -> 0%
where the time goes in v1:
time: 201 us; the launch traced here: 197 us
  starting transfers between devices  120 us (60%)
  waiting for transfers between devices  23.2 us (12%)
  matrix products  23.1 us (11%)
  other arithmetic  18.9 us (9%)
  between operations  6.12 us (3%)
  local copies, waits for them, and re-layouts  5.53 us (3%)
    ppermute x48, starting transfers between devices, moved(): lax.ppermute(value, 'fsdp', [(source, source + distance) for source in se...  96 us
    ppermute x48, waiting for transfers between devices, moved(): lax.ppermute(value, 'fsdp', [(source, source + distance) for source in se...  21.8 us
    ppermute x5, starting transfers between devices, swapped(): return lax.ppermute(value, axis, pairs)  19.4 us
    dot_general x16, matrix products, local(): jnp.dot(blocks[(members - i) % members], weight_blocks[i], preferred_elem...  17.4 us
    reduce_sum x8, other arithmetic, local(): jnp.sum(g * g)  11.9 us
    dot_general x16, matrix products, local(): lax.dot_general(block, residual, (((0,), (0,)), ((), ())), preferred_elem...  5.72 us
    ppermute x3, starting transfers between devices, local(): total = total + lax.ppermute(squares, 'fsdp', ring)  5.08 us
  transfers between devices with their start and end apart: 56, of which 12 were waited for; matrix products, arithmetic and copies ran while one was open for 19% of the time, Pallas kernels for 0%

profile of v1, /device:TPU:7, one launch (start us, length us, event | category | flops | bytes accessed | tf_op | source)
XLA Modules:
  0.0 197.2 jit_solution(15803947891600637123)
XLA Ops:
  0.0 1.9 copy.5
  3.1 3.9 %collective-permute-start.1 = (bf16[1024,128]{0,1:T(8,128)(2,1)}, bf16[1024,128]{0,1:T(8,128)(2,1)}, u32[]{:S(2)}, u32[]{:S(2)}) collective-permute-start(bf16[1024,128]{0,1:T(8,128)(2,1)} %get-tuple-element.20), channel_id=1, source_target_pairs={{0,1},{1,2},{2,3},{4,5},{5,6},{6,7},{8,9},{9,10},{10,11},{12,13},{... | collective-permute-start | bytes 786440 | tf_op jit(solution)/shard_map/ppermute | solution.py:21
  8.3 4.7 %collective-permute-start.13 = (bf16[1024,128]{0,1:T(8,128)(2,1)}, bf16[1024,128]{0,1:T(8,128)(2,1)}, u32[]{:S(2)}, u32[]{:S(2)}) collective-permute-start(bf16[1024,128]{0,1:T(8,128)(2,1)} %get-tuple-element.19), channel_id=1, source_target_pairs={{0,1},{1,2},{2,3},{4,5},{5,6},{6,7},{8,9},{9,10},{10,11},{12,13},{... | collective-permute-start | bytes 786440 | tf_op jit(solution)/shard_map/ppermute | solution.py:21
  14.3 4.7 %collective-permute-start.25 = (bf16[1024,128]{0,1:T(8,128)(2,1)}, bf16[1024,128]{0,1:T(8,128)(2,1)}, u32[]{:S(2)}, u32[]{:S(2)}) collective-permute-start(bf16[1024,128]{0,1:T(8,128)(2,1)} %get-tuple-element.17), channel_id=1, source_target_pairs={{0,1},{1,2},{2,3},{4,5},{5,6},{6,7},{8,9},{9,10},{10,11},{12,13},{... | collective-permute-start | bytes 786440 | tf_op jit(solution)/shard_map/ppermute | solution.py:21
  19.0 2.3 %fusion.58 = f32[448,128]{1,0:T(8,128)} fusion(bf16[1,448,4096]{2,1,0:T(8,128)(2,1)} %param.4, s32[]{:T(128)S(6)} %select_n.104, bf16[1024,512]{0,1:T(8,128)(2,1)S(1)} %bitcast_convert_fusion), kind=kOutput, calls=%fused_computation.88 | convolution fusion | flops 117440512 | bytes 1409028 | tf_op jit(solution)/shard_map/dot_general | solution.py:77
  21.3 2.3 %fusion.55 = f32[448,128]{1,0:T(8,128)} fusion(bf16[1,448,4096]{2,1,0:T(8,128)(2,1)} %param.4, s32[]{:T(128)S(6)} %select_n.104, bf16[1024,512]{0,1:T(8,128)(2,1)S(1)} %bitcast_convert_fusion), kind=kOutput, calls=%fused_computation.85 | convolution fusion | flops 117440512 | bytes 1409028 | tf_op jit(solution)/shard_map/dot_general | solution.py:77
  27.9 3.6 %collective-permute-done.3 = bf16[1024,128]{0,1:T(8,128)(2,1)} collective-permute-done((bf16[1024,128]{0,1:T(8,128)(2,1)}, bf16[1024,128]{0,1:T(8,128)(2,1)}, u32[]{:S(2)}, u32[]{:S(2)}) %collective-permute-start.3) | collective-permute-done | bytes 262176 | tf_op jit(solution)/shard_map/ppermute | solution.py:21
  43.1 4.4 %collective-permute-start.37 = (bf16[1024,128]{0,1:T(8,128)(2,1)S(1)}, bf16[1024,128]{0,1:T(8,128)(2,1)S(1)}, u32[]{:S(2)}, u32[]{:S(2)}) collective-permute-start(bf16[1024,128]{0,1:T(8,128)(2,1)S(1)} %copy-done.3), channel_id=1, source_target_pairs={{0,1},{1,2},{2,3},{4,5},{5,6},{6,7},{8,9},{9,10},{10,11},{12,13},{... | collective-permute-start | bytes 786440 | tf_op jit(solution)/shard_map/ppermute | solution.py:21
  58.7 5.4 %collective-permute-done.16 = bf16[1024,128]{0,1:T(8,128)(2,1)S(1)} collective-permute-done((bf16[1024,128]{0,1:T(8,128)(2,1)S(1)}, bf16[1024,128]{0,1:T(8,128)(2,1)S(1)}, u32[]{:S(2)}, u32[]{:S(2)}) %collective-permute-start.16) | collective-permute-done | bytes 262176 | tf_op jit(solution)/shard_map/ppermute | solution.py:21
  66.1 3.9 %collective-permute-done.27 = bf16[1024,128]{0,1:T(8,128)(2,1)S(1)} collective-permute-done((bf16[1024,128]{0,1:T(8,128)(2,1)S(1)}, bf16[1024,128]{0,1:T(8,128)(2,1)S(1)}, u32[]{:S(2)}, u32[]{:S(2)}) %collective-permute-start.27) | collective-permute-done | bytes 262176 | tf_op jit(solution)/shard_map/ppermute | solution.py:21
  70.0 6.1 %collective-permute-start = (f32[1024,512]{0,1:T(8,128)S(1)}, f32[1024,512]{0,1:T(8,128)}, u32[]{:S(2)}, u32[]{:S(2)}) collective-permute-start(f32[1024,512]{0,1:T(8,128)S(1)} %bitcast.104), channel_id=1, source_target_pairs={{0,4},{4,0},{8,12},{12,8},{16,20},{20,16},{24,28},{28,24},{1,5},{5... | collective-permute-start | bytes 6291464 | tf_op jit(solution)/shard_map/ppermute | solution.py:17
  82.2 4.3 %collective-permute-done.28 = bf16[1024,128]{0,1:T(8,128)(2,1)S(1)} collective-permute-done((bf16[1024,128]{0,1:T(8,128)(2,1)S(1)}, bf16[1024,128]{0,1:T(8,128)(2,1)S(1)}, u32[]{:S(2)}, u32[]{:S(2)}) %collective-permute-start.28) | collective-permute-done | bytes 262176 | tf_op jit(solution)/shard_map/ppermute | solution.py:21
  88.8 2.1 %collective-permute-start.7 = (bf16[1024,128]{0,1:T(8,128)(2,1)S(1)}, bf16[1024,128]{0,1:T(8,128)(2,1)S(1)}, u32[]{:S(2)}, u32[]{:S(2)}) collective-permute-start(bf16[1024,128]{0,1:T(8,128)(2,1)S(1)} %convolution_convert_fusion.14), channel_id=1, source_target_pairs={{0,1},{4,5},{8,9},{12,13},{16,17},{20,21},{24,25},{28,29}} | collective-permute-start | bytes 786440 | tf_op jit(solution)/shard_map/ppermute | solution.py:21
  96.6 3.3 %collective-permute-start.31 = (bf16[1024,128]{0,1:T(8,128)(2,1)S(1)}, bf16[1024,128]{0,1:T(8,128)(2,1)S(1)}, u32[]{:S(2)}, u32[]{:S(2)}) collective-permute-start(bf16[1024,128]{0,1:T(8,128)(2,1)S(1)} %convolution_convert_fusion.6), channel_id=1, source_target_pairs={{0,1},{4,5},{8,9},{12,13},{16,17},{20,21},{24,25},{28,29}} | collective-permute-start | bytes 786440 | tf_op jit(solution)/shard_map/ppermute | solution.py:21
  101.5 4.1 %collective-permute-start.43 = (bf16[1024,128]{0,1:T(8,128)(2,1)S(1)}, bf16[1024,128]{0,1:T(8,128)(2,1)S(1)}, u32[]{:S(2)}, u32[]{:S(2)}) collective-permute-start(bf16[1024,128]{0,1:T(8,128)(2,1)S(1)} %convolution_convert_fusion.2), channel_id=1, source_target_pairs={{0,1},{4,5},{8,9},{12,13},{16,17},{20,21},{24,25},{28,29}} | collective-permute-start | bytes 786440 | tf_op jit(solution)/shard_map/ppermute | solution.py:21
  107.8 4.7 %collective-permute-start.8 = (bf16[1024,128]{0,1:T(8,128)(2,1)S(1)}, bf16[1024,128]{0,1:T(8,128)(2,1)S(1)}, u32[]{:S(2)}, u32[]{:S(2)}) collective-permute-start(bf16[1024,128]{0,1:T(8,128)(2,1)S(1)} %get-tuple-element.25), channel_id=1, source_target_pairs={{0,1},{1,2},{4,5},{5,6},{8,9},{9,10},{12,13},{13,14},{16,17},{17,1... | collective-permute-start | bytes 786440 | tf_op jit(solution)/shard_map/ppermute | solution.py:21
  113.7 4.6 %collective-permute-start.20 = (bf16[1024,128]{0,1:T(8,128)(2,1)S(1)}, bf16[1024,128]{0,1:T(8,128)(2,1)S(1)}, u32[]{:S(2)}, u32[]{:S(2)}) collective-permute-start(bf16[1024,128]{0,1:T(8,128)(2,1)S(1)} %get-tuple-element.23), channel_id=1, source_target_pairs={{0,1},{1,2},{4,5},{5,6},{8,9},{9,10},{12,13},{13,14},{16,17},{17,1... | collective-permute-start | bytes 786440 | tf_op jit(solution)/shard_map/ppermute | solution.py:21
  119.4 4.6 %collective-permute-start.32 = (bf16[1024,128]{0,1:T(8,128)(2,1)S(1)}, bf16[1024,128]{0,1:T(8,128)(2,1)S(1)}, u32[]{:S(2)}, u32[]{:S(2)}) collective-permute-start(bf16[1024,128]{0,1:T(8,128)(2,1)S(1)} %get-tuple-element.21), channel_id=1, source_target_pairs={{0,1},{1,2},{4,5},{5,6},{8,9},{9,10},{12,13},{13,14},{16,17},{17,1... | collective-permute-start | bytes 786440 | tf_op jit(solution)/shard_map/ppermute | solution.py:21
  124.9 4.6 %collective-permute-start.44 = (bf16[1024,128]{0,1:T(8,128)(2,1)S(1)}, bf16[1024,128]{0,1:T(8,128)(2,1)S(1)}, u32[]{:S(2)}, u32[]{:S(2)}) collective-permute-start(bf16[1024,128]{0,1:T(8,128)(2,1)S(1)} %get-tuple-element.27), channel_id=1, source_target_pairs={{0,1},{1,2},{4,5},{5,6},{8,9},{9,10},{12,13},{13,14},{16,17},{17,1... | collective-permute-start | bytes 786440 | tf_op jit(solution)/shard_map/ppermute | solution.py:21
  131.0 4.6 %collective-permute-start.9 = (bf16[1024,128]{0,1:T(8,128)(2,1)S(1)}, bf16[1024,128]{0,1:T(8,128)(2,1)S(1)}, u32[]{:S(2)}, u32[]{:S(2)}) collective-permute-start(bf16[1024,128]{0,1:T(8,128)(2,1)S(1)} %add_convert_fusion.14), channel_id=1, source_target_pairs={{0,1},{1,2},{2,3},{4,5},{5,6},{6,7},{8,9},{9,10},{10,11},{12,13},{... | collective-permute-start | bytes 786440 | tf_op jit(solution)/shard_map/ppermute | solution.py:21
  137.1 4.0 %collective-permute-start.21 = (bf16[1024,128]{0,1:T(8,128)(2,1)S(1)}, bf16[1024,128]{0,1:T(8,128)(2,1)S(1)}, u32[]{:S(2)}, u32[]{:S(2)}) collective-permute-start(bf16[1024,128]{0,1:T(8,128)(2,1)S(1)} %add_convert_fusion.10), channel_id=1, source_target_pairs={{0,1},{1,2},{2,3},{4,5},{5,6},{6,7},{8,9},{9,10},{10,11},{12,13},{... | collective-permute-start | bytes 786440 | tf_op jit(solution)/shard_map/ppermute | solution.py:21
  142.5 4.0 %collective-permute-start.33 = (bf16[1024,128]{0,1:T(8,128)(2,1)S(1)}, bf16[1024,128]{0,1:T(8,128)(2,1)S(1)}, u32[]{:S(2)}, u32[]{:S(2)}) collective-permute-start(bf16[1024,128]{0,1:T(8,128)(2,1)S(1)} %add_convert_fusion.6), channel_id=1, source_target_pairs={{0,1},{1,2},{2,3},{4,5},{5,6},{6,7},{8,9},{9,10},{10,11},{12,13},{... | collective-permute-start | bytes 786440 | tf_op jit(solution)/shard_map/ppermute | solution.py:21
  148.6 4.0 %collective-permute-start.45 = (bf16[1024,128]{0,1:T(8,128)(2,1)S(1)}, bf16[1024,128]{0,1:T(8,128)(2,1)S(1)}, u32[]{:S(2)}, u32[]{:S(2)}) collective-permute-start(bf16[1024,128]{0,1:T(8,128)(2,1)S(1)} %add_convert_fusion.2), channel_id=1, source_target_pairs={{0,1},{1,2},{2,3},{4,5},{5,6},{6,7},{8,9},{9,10},{10,11},{12,13},{... | collective-permute-start | bytes 786440 | tf_op jit(solution)/shard_map/ppermute | solution.py:21
  153.4 11.7 %collective-permute-start.49 = (f32[1024,128]{0,1:T(8,128)S(1)}, f32[1024,128]{0,1:T(8,128)}, u32[]{:S(2)}, u32[]{:S(2)}) collective-permute-start(f32[1024,128]{0,1:T(8,128)S(1)} %get-tuple-element.12), channel_id=1, source_target_pairs={{0,4},{4,0},{8,12},{12,8},{16,20},{20,16},{24,28},{28,24},{1,5},{5... | collective-permute-start | bytes 1572872 | tf_op jit(solution)/shard_map/ppermute | solution.py:17
  172.4 1.8 multiply_reduce_fusion.3
  174.2 1.8 multiply_reduce_fusion.2
  177.3 1.8 multiply_reduce_fusion.1
  179.8 1.8 multiply_reduce_fusion
  182.3 4.3 %collective-permute-start.55 = (f32[2]{0:T(128)S(1)}, f32[2]{0:T(128)S(1)}, u32[]{:S(2)}, u32[]{:S(2)}) collective-permute-start(f32[2]{0:T(128)S(1)} %pad_maximum_fusion), channel_id=1, source_target_pairs={{0,3},{1,0},{2,1},{3,2},{4,7},{5,4},{6,5},{7,6},{8,11},{9,8},{10,9... | collective-permute-start | bytes 32 | tf_op jit(solution)/shard_map/ppermute | solution.py:104
  187.4 2.1 %add_multiply_fusion = f32[1024,512]{0,1:T(8,128)S(1)} fusion(f32[1024,512]{0,1:T(8,128)} %collective-permute-done, f32[1,1024,512]{1,2,0:T(8,128)S(1)} %copy.5), kind=kLoop, calls=%fused_computation.1 | loop fusion | flops 1048576 | bytes 6291456 | tf_op jit(solution)/shard_map/mul | solution.py:70
  191.4 3.8 %slice_subtract_fusion.3 = (f32[1024,128]{0,1:T(8,128)S(1)}, f32[1024,128]{0,1:T(8,128)S(1)}, f32[1024,128]{0,1:T(8,128)S(1)}, f32[1024,128]{0,1:T(8,128)S(1)}) fusion(f32[1024,512]{0,1:T(8,128)S(1)} %add_multiply_fusion, f32[1024,128]{0,1:T(8,128)} %collective-permute-done.49, f32[1024,128]{0,1:T(8,128)S(1)} %get-tuple-element.12, f32[]{:T(128)} %bitcast.10, ...), kind=kLoop, calls=%fused_computation.93 | loop fusion | flops 2621440 | bytes 8388616 | tf_op jit(solution)/shard_map/sub | solution.py:108
  195.4 1.8 copy.18
  (151 shorter events, 68.0 us)
Async XLA Ops:
  3.1 23.5 %collective-permute-start.1 = (bf16[1024,128]{0,1:T(8,128)(2,1)}, bf16[1024,128]{0,1:T(8,128)(2,1)}, u32[]{:S(2)}, u32[]{:S(2)}) collective-permute-start(bf16[1024,128]{0,1:T(8,128)(2,1)} %get-tuple-element.20), channel_id=1, source_target_pairs={{0,1},{1,2},{2,3},{4,5},{5,6},{6,7},{8,9},{9,10},{10,11},{12,13},{... | collective-permute-start | bytes 786440 | tf_op jit(solution)/shard_map/ppermute | solution.py:21
  7.0 16.6 %collective-permute-start.2 = (bf16[1024,128]{0,1:T(8,128)(2,1)}, bf16[1024,128]{0,1:T(8,128)(2,1)}, u32[]{:S(2)}, u32[]{:S(2)}) collective-permute-start(bf16[1024,128]{0,1:T(8,128)(2,1)} %get-tuple-element.20), channel_id=1, source_target_pairs={{1,0},{2,1},{3,2},{5,4},{6,5},{7,6},{9,8},{10,9},{11,10},{13,12},{... | collective-permute-start | bytes 786440 | tf_op jit(solution)/shard_map/ppermute | solution.py:21
  8.3 40.5 %collective-permute-start.13 = (bf16[1024,128]{0,1:T(8,128)(2,1)}, bf16[1024,128]{0,1:T(8,128)(2,1)}, u32[]{:S(2)}, u32[]{:S(2)}) collective-permute-start(bf16[1024,128]{0,1:T(8,128)(2,1)} %get-tuple-element.19), channel_id=1, source_target_pairs={{0,1},{1,2},{2,3},{4,5},{5,6},{6,7},{8,9},{9,10},{10,11},{12,13},{... | collective-permute-start | bytes 786440 | tf_op jit(solution)/shard_map/ppermute | solution.py:21
  13.0 21.7 %collective-permute-start.14 = (bf16[1024,128]{0,1:T(8,128)(2,1)}, bf16[1024,128]{0,1:T(8,128)(2,1)}, u32[]{:S(2)}, u32[]{:S(2)}) collective-permute-start(bf16[1024,128]{0,1:T(8,128)(2,1)} %get-tuple-element.19), channel_id=1, source_target_pairs={{1,0},{2,1},{3,2},{5,4},{6,5},{7,6},{9,8},{10,9},{11,10},{13,12},{... | collective-permute-start | bytes 786440 | tf_op jit(solution)/shard_map/ppermute | solution.py:21
  14.3 35.8 %collective-permute-start.25 = (bf16[1024,128]{0,1:T(8,128)(2,1)}, bf16[1024,128]{0,1:T(8,128)(2,1)}, u32[]{:S(2)}, u32[]{:S(2)}) collective-permute-start(bf16[1024,128]{0,1:T(8,128)(2,1)} %get-tuple-element.17), channel_id=1, source_target_pairs={{0,1},{1,2},{2,3},{4,5},{5,6},{6,7},{8,9},{9,10},{10,11},{12,13},{... | collective-permute-start | bytes 786440 | tf_op jit(solution)/shard_map/ppermute | solution.py:21
  34.7 19.3 %collective-permute-start.26 = (bf16[1024,128]{0,1:T(8,128)(2,1)}, bf16[1024,128]{0,1:T(8,128)(2,1)S(1)}, u32[]{:S(2)}, u32[]{:S(2)}) collective-permute-start(bf16[1024,128]{0,1:T(8,128)(2,1)} %get-tuple-element.17), channel_id=1, source_target_pairs={{1,0},{2,1},{3,2},{5,4},{6,5},{7,6},{9,8},{10,9},{11,10},{13,12},{... | collective-permute-start | bytes 786440 | tf_op jit(solution)/shard_map/ppermute | solution.py:21
  36.0 16.0 %collective-permute-start.15 = (bf16[1024,128]{0,1:T(8,128)(2,1)}, bf16[1024,128]{0,1:T(8,128)(2,1)S(1)}, u32[]{:S(2)}, u32[]{:S(2)}) collective-permute-start(bf16[1024,128]{0,1:T(8,128)(2,1)} %collective-permute-done.14), channel_id=1, source_target_pairs={{1,0},{2,1},{5,4},{6,5},{9,8},{10,9},{13,12},{14,13},{17,16},{18,1... | collective-permute-start | bytes 786440 | tf_op jit(solution)/shard_map/ppermute | solution.py:21
  43.1 12.3 %collective-permute-start.37 = (bf16[1024,128]{0,1:T(8,128)(2,1)S(1)}, bf16[1024,128]{0,1:T(8,128)(2,1)S(1)}, u32[]{:S(2)}, u32[]{:S(2)}) collective-permute-start(bf16[1024,128]{0,1:T(8,128)(2,1)S(1)} %copy-done.3), channel_id=1, source_target_pairs={{0,1},{1,2},{2,3},{4,5},{5,6},{6,7},{8,9},{9,10},{10,11},{12,13},{... | collective-permute-start | bytes 786440 | tf_op jit(solution)/shard_map/ppermute | solution.py:21
  52.0 12.1 %collective-permute-start.16 = (bf16[1024,128]{0,1:T(8,128)(2,1)S(1)}, bf16[1024,128]{0,1:T(8,128)(2,1)S(1)}, u32[]{:S(2)}, u32[]{:S(2)}) collective-permute-start(bf16[1024,128]{0,1:T(8,128)(2,1)S(1)} %collective-permute-done.15), channel_id=1, source_target_pairs={{1,0},{5,4},{9,8},{13,12},{17,16},{21,20},{25,24},{29,28}} | collective-permute-start | bytes 786440 | tf_op jit(solution)/shard_map/ppermute | solution.py:21
  54.0 16.0 %collective-permute-start.27 = (bf16[1024,128]{0,1:T(8,128)(2,1)S(1)}, bf16[1024,128]{0,1:T(8,128)(2,1)S(1)}, u32[]{:S(2)}, u32[]{:S(2)}) collective-permute-start(bf16[1024,128]{0,1:T(8,128)(2,1)S(1)} %collective-permute-done.26), channel_id=1, source_target_pairs={{1,0},{2,1},{5,4},{6,5},{9,8},{10,9},{13,12},{14,13},{17,16},{18,1... | collective-permute-start | bytes 786440 | tf_op jit(solution)/shard_map/ppermute | solution.py:21
  55.3 20.7 %collective-permute-start.29 = (bf16[1024,128]{0,1:T(8,128)(2,1)}, bf16[1024,128]{0,1:T(8,128)(2,1)S(1)}, u32[]{:S(2)}, u32[]{:S(2)}) collective-permute-start(bf16[1024,128]{0,1:T(8,128)(2,1)} %collective-permute-done.25), channel_id=1, source_target_pairs={{1,2},{2,3},{5,6},{6,7},{9,10},{10,11},{13,14},{14,15},{17,18},{18... | collective-permute-start | bytes 786440 | tf_op jit(solution)/shard_map/ppermute | solution.py:21
  56.8 20.6 %collective-permute-start.39 = (bf16[1024,128]{0,1:T(8,128)(2,1)S(1)}, bf16[1024,128]{0,1:T(8,128)(2,1)S(1)}, u32[]{:S(2)}, u32[]{:S(2)}) collective-permute-start(bf16[1024,128]{0,1:T(8,128)(2,1)S(1)} %collective-permute-done.38), channel_id=1, source_target_pairs={{1,0},{2,1},{5,4},{6,5},{9,8},{10,9},{13,12},{14,13},{17,16},{18,1... | collective-permute-start | bytes 786440 | tf_op jit(solution)/shard_map/ppermute | solution.py:21
  58.1 20.0 %collective-permute-start.41 = (bf16[1024,128]{0,1:T(8,128)(2,1)S(1)}, bf16[1024,128]{0,1:T(8,128)(2,1)S(1)}, u32[]{:S(2)}, u32[]{:S(2)}) collective-permute-start(bf16[1024,128]{0,1:T(8,128)(2,1)S(1)} %collective-permute-done.37), channel_id=1, source_target_pairs={{1,2},{2,3},{5,6},{6,7},{9,10},{10,11},{13,14},{14,15},{17,18},{18... | collective-permute-start | bytes 786440 | tf_op jit(solution)/shard_map/ppermute | solution.py:21
  64.2 15.2 %collective-permute-start.18 = (bf16[1024,128]{0,1:T(8,128)(2,1)S(1)}, bf16[1024,128]{0,1:T(8,128)(2,1)S(1)}, u32[]{:S(2)}, u32[]{:S(2)}) collective-permute-start(bf16[1024,128]{0,1:T(8,128)(2,1)S(1)} %collective-permute-done.17), channel_id=1, source_target_pairs={{2,3},{6,7},{10,11},{14,15},{18,19},{22,23},{26,27},{30,31}} | collective-permute-start | bytes 786440 | tf_op jit(solution)/shard_map/ppermute | solution.py:21
  70.0 117.4 %collective-permute-start = (f32[1024,512]{0,1:T(8,128)S(1)}, f32[1024,512]{0,1:T(8,128)}, u32[]{:S(2)}, u32[]{:S(2)}) collective-permute-start(f32[1024,512]{0,1:T(8,128)S(1)} %bitcast.104), channel_id=1, source_target_pairs={{0,4},{4,0},{8,12},{12,8},{16,20},{20,16},{24,28},{28,24},{1,5},{5... | collective-permute-start | bytes 6291464 | tf_op jit(solution)/shard_map/ppermute | solution.py:17
  78.1 14.0 %collective-permute-start.40 = (bf16[1024,128]{0,1:T(8,128)(2,1)S(1)}, bf16[1024,128]{0,1:T(8,128)(2,1)S(1)}, u32[]{:S(2)}, u32[]{:S(2)}) collective-permute-start(bf16[1024,128]{0,1:T(8,128)(2,1)S(1)} %collective-permute-done.39), channel_id=1, source_target_pairs={{1,0},{5,4},{9,8},{13,12},{17,16},{21,20},{25,24},{29,28}} | collective-permute-start | bytes 786440 | tf_op jit(solution)/shard_map/ppermute | solution.py:21
  79.4 13.5 %collective-permute-start.42 = (bf16[1024,128]{0,1:T(8,128)(2,1)S(1)}, bf16[1024,128]{0,1:T(8,128)(2,1)S(1)}, u32[]{:S(2)}, u32[]{:S(2)}) collective-permute-start(bf16[1024,128]{0,1:T(8,128)(2,1)S(1)} %collective-permute-done.41), channel_id=1, source_target_pairs={{2,3},{6,7},{10,11},{14,15},{18,19},{22,23},{26,27},{30,31}} | collective-permute-start | bytes 786440 | tf_op jit(solution)/shard_map/ppermute | solution.py:21
  101.5 11.4 %collective-permute-start.43 = (bf16[1024,128]{0,1:T(8,128)(2,1)S(1)}, bf16[1024,128]{0,1:T(8,128)(2,1)S(1)}, u32[]{:S(2)}, u32[]{:S(2)}) collective-permute-start(bf16[1024,128]{0,1:T(8,128)(2,1)S(1)} %convolution_convert_fusion.2), channel_id=1, source_target_pairs={{0,1},{4,5},{8,9},{12,13},{16,17},{20,21},{24,25},{28,29}} | collective-permute-start | bytes 786440 | tf_op jit(solution)/shard_map/ppermute | solution.py:21
  107.2 11.5 %collective-permute-start.11 = (bf16[1024,128]{0,1:T(8,128)(2,1)S(1)}, bf16[1024,128]{0,1:T(8,128)(2,1)S(1)}, u32[]{:S(2)}, u32[]{:S(2)}) collective-permute-start(bf16[1024,128]{0,1:T(8,128)(2,1)S(1)} %get-tuple-element.26), channel_id=1, source_target_pairs={{2,1},{3,2},{6,5},{7,6},{10,9},{11,10},{14,13},{15,14},{18,17},{19... | collective-permute-start | bytes 786440 | tf_op jit(solution)/shard_map/ppermute | solution.py:21
  107.8 11.6 %collective-permute-start.8 = (bf16[1024,128]{0,1:T(8,128)(2,1)S(1)}, bf16[1024,128]{0,1:T(8,128)(2,1)S(1)}, u32[]{:S(2)}, u32[]{:S(2)}) collective-permute-start(bf16[1024,128]{0,1:T(8,128)(2,1)S(1)} %get-tuple-element.25), channel_id=1, source_target_pairs={{0,1},{1,2},{4,5},{5,6},{8,9},{9,10},{12,13},{13,14},{16,17},{17,1... | collective-permute-start | bytes 786440 | tf_op jit(solution)/shard_map/ppermute | solution.py:21
  119.4 11.5 %collective-permute-start.32 = (bf16[1024,128]{0,1:T(8,128)(2,1)S(1)}, bf16[1024,128]{0,1:T(8,128)(2,1)S(1)}, u32[]{:S(2)}, u32[]{:S(2)}) collective-permute-start(bf16[1024,128]{0,1:T(8,128)(2,1)S(1)} %get-tuple-element.21), channel_id=1, source_target_pairs={{0,1},{1,2},{4,5},{5,6},{8,9},{9,10},{12,13},{13,14},{16,17},{17,1... | collective-permute-start | bytes 786440 | tf_op jit(solution)/shard_map/ppermute | solution.py:21
  124.1 11.6 %collective-permute-start.47 = (bf16[1024,128]{0,1:T(8,128)(2,1)S(1)}, bf16[1024,128]{0,1:T(8,128)(2,1)S(1)}, u32[]{:S(2)}, u32[]{:S(2)}) collective-permute-start(bf16[1024,128]{0,1:T(8,128)(2,1)S(1)} %get-tuple-element.28), channel_id=1, source_target_pairs={{2,1},{3,2},{6,5},{7,6},{10,9},{11,10},{14,13},{15,14},{18,17},{19... | collective-permute-start | bytes 786440 | tf_op jit(solution)/shard_map/ppermute | solution.py:21
  124.9 12.2 %collective-permute-start.44 = (bf16[1024,128]{0,1:T(8,128)(2,1)S(1)}, bf16[1024,128]{0,1:T(8,128)(2,1)S(1)}, u32[]{:S(2)}, u32[]{:S(2)}) collective-permute-start(bf16[1024,128]{0,1:T(8,128)(2,1)S(1)} %get-tuple-element.27), channel_id=1, source_target_pairs={{0,1},{1,2},{4,5},{5,6},{8,9},{9,10},{12,13},{13,14},{16,17},{17,1... | collective-permute-start | bytes 786440 | tf_op jit(solution)/shard_map/ppermute | solution.py:21
  129.6 11.6 %collective-permute-start.12 = (bf16[1024,128]{0,1:T(8,128)(2,1)S(1)}, bf16[1024,128]{0,1:T(8,128)(2,1)S(1)}, u32[]{:S(2)}, u32[]{:S(2)}) collective-permute-start(bf16[1024,128]{0,1:T(8,128)(2,1)S(1)} %add_convert_fusion.12), channel_id=1, source_target_pairs={{1,0},{2,1},{3,2},{5,4},{6,5},{7,6},{9,8},{10,9},{11,10},{13,12},{... | collective-permute-start | bytes 786440 | tf_op jit(solution)/shard_map/ppermute | solution.py:21
  131.0 11.5 %collective-permute-start.9 = (bf16[1024,128]{0,1:T(8,128)(2,1)S(1)}, bf16[1024,128]{0,1:T(8,128)(2,1)S(1)}, u32[]{:S(2)}, u32[]{:S(2)}) collective-permute-start(bf16[1024,128]{0,1:T(8,128)(2,1)S(1)} %add_convert_fusion.14), channel_id=1, source_target_pairs={{0,1},{1,2},{2,3},{4,5},{5,6},{6,7},{8,9},{9,10},{10,11},{12,13},{... | collective-permute-start | bytes 786440 | tf_op jit(solution)/shard_map/ppermute | solution.py:21
  135.7 11.6 %collective-permute-start.24 = (bf16[1024,128]{0,1:T(8,128)(2,1)S(1)}, bf16[1024,128]{0,1:T(8,128)(2,1)S(1)}, u32[]{:S(2)}, u32[]{:S(2)}) collective-permute-start(bf16[1024,128]{0,1:T(8,128)(2,1)S(1)} %add_convert_fusion.8), channel_id=1, source_target_pairs={{1,0},{2,1},{3,2},{5,4},{6,5},{7,6},{9,8},{10,9},{11,10},{13,12},{... | collective-permute-start | bytes 786440 | tf_op jit(solution)/shard_map/ppermute | solution.py:21
  137.1 11.5 %collective-permute-start.21 = (bf16[1024,128]{0,1:T(8,128)(2,1)S(1)}, bf16[1024,128]{0,1:T(8,128)(2,1)S(1)}, u32[]{:S(2)}, u32[]{:S(2)}) collective-permute-start(bf16[1024,128]{0,1:T(8,128)(2,1)S(1)} %add_convert_fusion.10), channel_id=1, source_target_pairs={{0,1},{1,2},{2,3},{4,5},{5,6},{6,7},{8,9},{9,10},{10,11},{12,13},{... | collective-permute-start | bytes 786440 | tf_op jit(solution)/shard_map/ppermute | solution.py:21
  141.2 12.2 %collective-permute-start.36 = (bf16[1024,128]{0,1:T(8,128)(2,1)S(1)}, bf16[1024,128]{0,1:T(8,128)(2,1)S(1)}, u32[]{:S(2)}, u32[]{:S(2)}) collective-permute-start(bf16[1024,128]{0,1:T(8,128)(2,1)S(1)} %add_convert_fusion.4), channel_id=1, source_target_pairs={{1,0},{2,1},{3,2},{5,4},{6,5},{7,6},{9,8},{10,9},{11,10},{13,12},{... | collective-permute-start | bytes 786440 | tf_op jit(solution)/shard_map/ppermute | solution.py:21
  142.5 22.6 %collective-permute-start.33 = (bf16[1024,128]{0,1:T(8,128)(2,1)S(1)}, bf16[1024,128]{0,1:T(8,128)(2,1)S(1)}, u32[]{:S(2)}, u32[]{:S(2)}) collective-permute-start(bf16[1024,128]{0,1:T(8,128)(2,1)S(1)} %add_convert_fusion.6), channel_id=1, source_target_pairs={{0,1},{1,2},{2,3},{4,5},{5,6},{6,7},{8,9},{9,10},{10,11},{12,13},{... | collective-permute-start | bytes 786440 | tf_op jit(solution)/shard_map/ppermute | solution.py:21
  147.3 19.4 %collective-permute-start.48 = (bf16[1024,128]{0,1:T(8,128)(2,1)S(1)}, bf16[1024,128]{0,1:T(8,128)(2,1)S(1)}, u32[]{:S(2)}, u32[]{:S(2)}) collective-permute-start(bf16[1024,128]{0,1:T(8,128)(2,1)S(1)} %add_convert_fusion), channel_id=1, source_target_pairs={{1,0},{2,1},{3,2},{5,4},{6,5},{7,6},{9,8},{10,9},{11,10},{13,12},{... | collective-permute-start | bytes 786440 | tf_op jit(solution)/shard_map/ppermute | solution.py:21
  148.6 18.6 %collective-permute-start.45 = (bf16[1024,128]{0,1:T(8,128)(2,1)S(1)}, bf16[1024,128]{0,1:T(8,128)(2,1)S(1)}, u32[]{:S(2)}, u32[]{:S(2)}) collective-permute-start(bf16[1024,128]{0,1:T(8,128)(2,1)S(1)} %add_convert_fusion.2), channel_id=1, source_target_pairs={{0,1},{1,2},{2,3},{4,5},{5,6},{6,7},{8,9},{9,10},{10,11},{12,13},{... | collective-permute-start | bytes 786440 | tf_op jit(solution)/shard_map/ppermute | solution.py:21
  153.4 19.0 %collective-permute-start.49 = (f32[1024,128]{0,1:T(8,128)S(1)}, f32[1024,128]{0,1:T(8,128)}, u32[]{:S(2)}, u32[]{:S(2)}) collective-permute-start(f32[1024,128]{0,1:T(8,128)S(1)} %get-tuple-element.12), channel_id=1, source_target_pairs={{0,4},{4,0},{8,12},{12,8},{16,20},{20,16},{24,28},{28,24},{1,5},{5... | collective-permute-start | bytes 1572872 | tf_op jit(solution)/shard_map/ppermute | solution.py:17
  (29 other events, 292.2 us)

commit v2 on v0

v2 whole, which is shorter than its diff:
```python
import functools

import jax
import jax.numpy as jnp
from jax import lax
from jax.experimental import pallas as pl
from jax.experimental.pallas import tpu as pltpu
from jax.sharding import PartitionSpec as P

SLOT = 64
STEP = 3
ALIGN = 16
MORE = 32

learning_rate = 0.1
epsilon = 1e-06


def swapped(value, axis, bit):
    mask = 2**bit
    pairs = [(source, source ^ mask) for source in range(lax.axis_size(axis))]
    return lax.ppermute(value, axis, pairs)


def turned(value, distance):
    members = lax.axis_size("fsdp")
    ring = [(source, (source + distance) % members) for source in range(members)]
    return lax.ppermute(value, "fsdp", ring)


def live_before(lengths_ref, sequence):
    total = jnp.int32(0)
    for q in range(lengths_ref.shape[1]):
        total = total + jnp.where(q < sequence, lengths_ref[0, q], 0)
    return total


def aligned(place):
    return pl.multiple_of(place // ALIGN * ALIGN, ALIGN)


def picking(lengths_ref, member, rows, tokens):
    sequences = tokens // SLOT
    place = live_before(lengths_ref, member * sequences) % ALIGN
    slot = lax.broadcasted_iota(jnp.int32, (1, tokens), 1)
    places = jnp.full((1, tokens), -1, jnp.int32)
    for s in range(sequences):
        length = lengths_ref[0, member * sequences + s]
        position = slot - s * SLOT
        places = jnp.where((position >= 0) & (position < length), position + place, places)
        place = place + length
    row = lax.broadcasted_iota(jnp.int32, (rows, tokens), 0)
    return jnp.where(row == places, 1.0, 0.0).astype(jnp.bfloat16)


def compact_kernel(first, index_ref, lengths_ref, features_ref, *refs):
    others = (len(refs) - 3) // 2
    outs, (choice_ref, blocks_ref, sems) = refs[: 2 * others], refs[2 * others :]
    index = index_ref[0]
    members = others + 1
    tokens, local_rows = blocks_ref.shape[1:]
    copies = []
    for i in range(others):
        owner = lax.rem(index + i + 1, members)
        columns = pl.ds(pl.multiple_of(owner * local_rows, 128), local_rows)
        copies.append(
            pltpu.make_async_copy(features_ref.at[:, columns], blocks_ref.at[i], sems.at[i])
        )
        copies[-1].start()
    more = outs[1].shape[0]
    longest = jnp.int32(0)
    before = jnp.int32(0)
    sequences = tokens // SLOT
    for member in range(members):
        after = before
        for q in range(sequences):
            after = after + lengths_ref[0, member * sequences + q]
        longest = jnp.maximum(longest, after - aligned(before))
        before = after
    choice = jnp.int32(0)
    for size in more_sizes(more)[:-1]:
        choice = choice + jnp.where(longest > first + size, 1, 0)
    choice_ref[0] = choice
    pick = picking(lengths_ref, index, first + more, tokens)
    width = min(256, local_rows)
    for i in range(others):
        copies[i].wait()

        @pl.loop(0, local_rows // width)
        def _(j, i=i):
            columns = pl.ds(pl.multiple_of(j * width, width), width)
            rows = jnp.dot(pick, blocks_ref[i, :, columns], preferred_element_type=jnp.float32)
            rows = rows.astype(jnp.bfloat16)
            outs[2 * i][:, columns] = rows[:first]
            outs[2 * i + 1][:, columns] = rows[first:]


def own_kernel(
    scale,
    index_ref,
    lengths_ref,
    features_ref,
    targets_ref,
    master_ref,
    partner_ref,
    first_ref,
    more_ref,
    keys_ref,
    low_ref,
    halves_ref,
    block_ref,
    sem,
):
    index = index_ref[0]
    tokens, local_rows = block_ref.shape
    columns = pl.ds(pl.multiple_of(index * local_rows, 128), local_rows)
    copy = pltpu.make_async_copy(features_ref.at[:, columns], block_ref, sem)
    copy.start()
    first, more = first_ref.shape[0], more_ref.shape[0]
    low_ref[...] = master_ref[...].astype(jnp.bfloat16)
    halves_ref[...] = 0.5 * (master_ref[...] + partner_ref[...])
    pick = picking(lengths_ref, index, first + more, tokens)
    copy.wait()
    rows = jnp.dot(pick, block_ref[...], preferred_element_type=jnp.float32).astype(jnp.bfloat16)
    first_ref[...] = rows[:first]
    more_ref[...] = rows[first:]
    keys_ref[...] = jnp.dot(
        rows, low_ref[...], preferred_element_type=jnp.float32
    ) * scale - jnp.dot(pick, targets_ref[...], preferred_element_type=jnp.float32)


def keys_kernel(members, scale, index_ref, lengths_ref, keys_ref, low_ref, *refs):
    held, sums, total_ref = refs[: 2 * members - 2], refs[2 * members - 2 : -1], refs[-1]
    index = index_ref[0]
    sequences = lengths_ref.shape[1] // members
    share = sums[0].shape[0]
    total_ref[...] = jnp.zeros_like(total_ref)
    own_start = aligned(live_before(lengths_ref, index * sequences))
    total_ref[pl.ds(own_start, keys_ref.shape[0])] = keys_ref[...]
    for i in range(1, members):
        member = lax.rem(index + members - i, members)
        end = live_before(lengths_ref, (member + 1) * sequences)
        start = aligned(live_before(lengths_ref, member * sequences))
        first_ref, more_ref = held[2 * i - 2 : 2 * i]
        first = first_ref.shape[0]

        def add(ref, offset, start=start):
            total_ref[pl.ds(start + offset, ref.shape[0])] += (
                jnp.dot(ref[...], low_ref[...], preferred_element_type=jnp.float32) * scale
            )

        add(first_ref, 0)
        pl.when(end - start > first)(functools.partial(add, more_ref, first))
    for i in range(members):
        owner = lax.rem(index + i, members)
        block = total_ref[pl.ds(pl.multiple_of(owner * share, ALIGN), share)]
        sums[i][...] = block.astype(sums[i].dtype)


def gradient_kernel(members, index_ref, lengths_ref, *refs):
    residuals, held = refs[:members], refs[members : 3 * members]
    gradient_ref, low_ref, squares_ref, all_ref = refs[3 * members :]
    index = index_ref[0]
    share = residuals[0].shape[0]
    first, more = held[0].shape[0], held[1].shape[0]
    sequences = lengths_ref.shape[1] // members
    rest = first + more
    all_ref[pl.ds(members * share, rest)] = jnp.zeros((rest, all_ref.shape[1]), all_ref.dtype)
    for i in range(members):
        owner = lax.rem(index + members - i, members)
        all_ref[pl.ds(pl.multiple_of(owner * share, ALIGN), share)] = residuals[i][...]
    for i in range(members):
        member = lax.rem(index + members - i, members)
        end = live_before(lengths_ref, (member + 1) * sequences)
        start = aligned(live_before(lengths_ref, member * sequences))

        def product(ref, offset, start=start):
            return lax.dot_general(
                ref[...],
                all_ref[pl.ds(start + offset, ref.shape[0])],
                (((0,), (0,)), ((), ())),
                preferred_element_type=jnp.float32,
            )

        def add_more(product=product, ref=held[2 * i + 1]):
            gradient_ref[...] += product(ref, first)

        if i:
            gradient_ref[...] += product(held[2 * i], 0)
        else:
            gradient_ref[...] = product(held[2 * i], 0)
        pl.when(end - start > first)(add_more)
    gradient = gradient_ref[...]
    low_ref[...] = gradient.astype(low_ref.dtype)
    squares = jnp.sum((gradient * gradient).reshape(-1, 8, gradient.shape[1]), axis=0)
    lanes = squares.shape[1] // 128
    squares_ref[...] = sum(squares[:, 128 * j : 128 * (j + 1)] for j in range(lanes))


def average_kernel(entries, own_ref, other_ref, halves_ref, gradient_ref, partner_ref, out_ref):
    half = 0.5 * learning_rate
    own = half * lax.rsqrt(jnp.sum(own_ref[...], keepdims=True) / entries + epsilon)
    other = half * lax.rsqrt(jnp.sum(other_ref[...], keepdims=True) / entries + epsilon)
    out_ref[...] = (
        halves_ref[...]
        - gradient_ref[...] * own
        - partner_ref[...].astype(jnp.float32) * other
    )


def more_sizes(more):
    return [0] + [size for size in (32, 64, 96) if size < more] + [more]


def more_rows(size, blocks):
    members = lax.axis_size("fsdp")
    if size == 0:
        return [jnp.zeros_like(block) for block in blocks]
    moved = [turned(blocks[i - 1][:size], i) for i in range(1, members)]
    return [jnp.pad(m, ((0, b.shape[0] - size), (0, 0))) for m, b in zip(moved, blocks)]


def local(activations, targets, weights, lengths):
    features = activations[0]
    wanted = targets[0]
    master = weights[0]
    tokens_here = features.shape[0]
    local_rows, columns = master.shape
    members = lax.axis_size("fsdp")
    index = lax.axis_index("fsdp")
    distance_bit = STEP % (lax.axis_size("replica").bit_length() - 1)
    share = tokens_here // 2
    first = -(-(share + 64) // MORE) * MORE
    more = -(-(tokens_here + ALIGN - first) // MORE) * MORE
    scale = features.shape[1] ** (-0.5)

    vmem = pl.BlockSpec(memory_space=pltpu.VMEM)
    anywhere = pl.BlockSpec(memory_space=pl.ANY)
    smem = pl.BlockSpec(memory_space=pltpu.SMEM)
    params = pltpu.CompilerParams(vmem_limit_bytes=40 * 2**20)
    scalars = jnp.stack([index, index])
    first_shape = jax.ShapeDtypeStruct((first, local_rows), jnp.bfloat16)
    more_shape = jax.ShapeDtypeStruct((more, local_rows), jnp.bfloat16)

    partner_master = swapped(master, "replica", distance_bit)

    *sent, choice = pl.pallas_call(
        functools.partial(compact_kernel, first),
        in_specs=[smem, smem, anywhere],
        out_specs=[vmem] * (2 * members - 2) + [smem],
        out_shape=[first_shape, more_shape] * (members - 1) + [jax.ShapeDtypeStruct((1,), jnp.int32)],
        scratch_shapes=[
            pltpu.VMEM((members - 1, tokens_here, local_rows), jnp.bfloat16),
            pltpu.SemaphoreType.DMA((members - 1,)),
        ],
        compiler_params=pltpu.CompilerParams(vmem_limit_bytes=56 * 2**20),
    )(scalars, lengths, features)

    held_first = [turned(sent[2 * i - 2], i) for i in range(1, members)]
    held_more = lax.switch(
        choice[0], [functools.partial(more_rows, size) for size in more_sizes(more)], sent[1::2]
    )
    held = [array for pair in zip(held_first, held_more) for array in pair]

    own_first, own_more, own_keys, low, halves = pl.pallas_call(
        functools.partial(own_kernel, scale),
        in_specs=[smem, smem, anywhere, vmem, vmem, vmem],
        out_specs=[vmem] * 5,
        out_shape=[
            first_shape,
            more_shape,
            jax.ShapeDtypeStruct((first + more, columns), jnp.float32),
            jax.ShapeDtypeStruct((local_rows, columns), jnp.bfloat16),
            jax.ShapeDtypeStruct((local_rows, columns), jnp.float32),
        ],
        scratch_shapes=[
            pltpu.VMEM((tokens_here, local_rows), jnp.bfloat16),
            pltpu.SemaphoreType.DMA,
        ],
        compiler_params=params,
        cost_estimate=pl.CostEstimate(
            flops=2 * (first + more) * local_rows * (tokens_here + columns),
            bytes_accessed=20 * local_rows * columns,
            transcendentals=0,
        ),
    )(scalars, lengths, features, wanted, master, partner_master)

    sums = pl.pallas_call(
        functools.partial(keys_kernel, members, scale),
        in_specs=[smem, smem, vmem, vmem] + [vmem] * (2 * members - 2),
        out_specs=[vmem] * members,
        out_shape=[
            jax.ShapeDtypeStruct((share, columns), jnp.bfloat16 if i else jnp.float32)
            for i in range(members)
        ],
        scratch_shapes=[pltpu.VMEM((members * share + first + more, columns), jnp.float32)],
        compiler_params=params,
    )(scalars, lengths, own_keys, low, *held)

    residual = sums[0]
    for i in range(1, members):
        residual = residual + turned(sums[i], i).astype(jnp.float32)
    residual = residual.astype(jnp.bfloat16)
    residuals = [residual] + [turned(residual, i) for i in range(1, members)]

    gradient, low_gradient, squares = pl.pallas_call(
        functools.partial(gradient_kernel, members),
        in_specs=[smem, smem] + [vmem] * (3 * members),
        out_specs=[vmem] * 3,
        out_shape=[
            jax.ShapeDtypeStruct((local_rows, columns), jnp.float32),
            jax.ShapeDtypeStruct((local_rows, columns), jnp.bfloat16),
            jax.ShapeDtypeStruct((8, 128), jnp.float32),
        ],
        scratch_shapes=[pltpu.VMEM((members * share + first + more, columns), jnp.bfloat16)],
        compiler_params=params,
    )(scalars, lengths, *residuals, own_first, own_more, *held)

    partner_gradient = swapped(low_gradient, "replica", distance_bit)
    total = squares
    for i in range(1, members):
        total = total + turned(squares, i)
    partner_total = swapped(total, "replica", distance_bit)

    rows = min(256, local_rows)
    whole = pl.BlockSpec((8, 128), lambda j: (0, 0))
    tile = pl.BlockSpec((rows, columns), lambda j: (j, 0))
    averaged = pl.pallas_call(
        functools.partial(average_kernel, members * local_rows * columns),
        grid=(local_rows // rows,),
        in_specs=[whole, whole, tile, tile, tile],
        out_specs=tile,
        out_shape=jax.ShapeDtypeStruct((local_rows, columns), jnp.float32),
    )(total, partner_total, halves, gradient, partner_gradient)
    return averaged[None]


def solution(mesh):
    return jax.shard_map(
        local,
        mesh=mesh,
        in_specs=(
            P("replica", "fsdp", None),
            P("replica", "fsdp", None),
            P("replica", "fsdp", None),
            P("replica", None),
        ),
        out_specs=P("replica", "fsdp", None),
        check_vma=False,
    )
```

time: 209 us -> 144 us (0.69)
  the two profiles are of different devices: /device:TPU:7 before, /device:TPU:0 now
where the time goes in v2:
time: 144 us; the launch traced here: 142 us
  waiting for transfers between devices  71.7 us (50%)
  starting transfers between devices  37.6 us (26%)
  Pallas kernels  23.2 us (16%)
  local copies, waits for them, and re-layouts  8.14 us (6%)
    ppermute x15, waiting for transfers between devices, turned(): return lax.ppermute(value, 'fsdp', ring)  70.5 us
    ppermute x15, starting transfers between devices, turned(): return lax.ppermute(value, 'fsdp', ring)  37.1 us
    pallas_call x1, Pallas kernels, local(): pl.pallas_call(functools.partial(compact_kernel, first), in_specs=[smem,...  6.41 us
    unnamed x20, local copies, waits for them, and re-layouts  5.75 us
    pallas_call x1, Pallas kernels, local(): pl.pallas_call(functools.partial(gradient_kernel, members), in_specs=[sme...  5.04 us
    pallas_call x1, Pallas kernels, local(): pl.pallas_call(functools.partial(average_kernel, members * local_rows * c...  4.84 us
    pallas_call x1, Pallas kernels, local(): pl.pallas_call(functools.partial(own_kernel, scale), in_specs=[smem, smem...  3.57 us
    pallas_call x1, Pallas kernels, local(): pl.pallas_call(functools.partial(keys_kernel, members, scale), in_specs=[...  3.32 us
  transfers between devices with their start and end apart: 18, of which 11 were waited for; matrix products, arithmetic and copies ran while one was open for 2% of the time, Pallas kernels for 7%

profile of v2, /device:TPU:0, one launch (start us, length us, event | category | flops | bytes accessed | tf_op | source)
XLA Modules:
  0.0 142.1 jit_solution(15780844673926347058)
XLA Ops:
  1.1 6.4 %shard_map.47 = (bf16[288,1024]{1,0:T(8,128)(2,1)}, bf16[192,1024]{1,0:T(8,128)(2,1)S(1)}, bf16[288,1024]{1,0:T(8,128)(2,1)}, bf16[192,1024]{1,0:T(8,128)(2,1)S(...) custom-call(s32[2]{0:T(128)} %pad_add_fusion.index_ref, s32[1,28]{1,0:T(1,128)} %lengths_ref.7, ...), custom_call_target="tpu_custom_call" | custom-call | tf_op jit(solution)/shard_map/pallas_call | solution.py:247
  7.5 2.6 %collective-permute-start.13 = (bf16[288,1024]{1,0:T(8,128)(2,1)}, bf16[288,1024]{1,0:T(8,128)(2,1)S(1)}, u32[]{:S(2)}, u32[]{:S(2)}) collective-permute-start(bf16[288,1024]{1,0:T(8,128)(2,1)} %get-tuple-element.65), channel_id=1, source_target_pairs={{0,1},{1,2},{2,3},{3,0},{4,5},{5,6},{6,7},{7,4},{8,9},{9,10},{10,1... | collective-permute-start | bytes 1769480 | tf_op jit(solution)/shard_map/ppermute | solution.py:28
  10.8 24.2 %conditional.1 = (bf16[192,1024]{1,0:T(8,128)(2,1)}, bf16[192,1024]{1,0:T(8,128)(2,1)}, bf16[192,1024]{1,0:T(8,128)(2,1)}) conditional(s32[]{:T(128)} %bitcast.4, () %tuple.25, (bf16[192,1024]{1,0:T(8,128)(2,1)S(1)}, bf16[192,1024]{1,0:T(8,128)(2,1)S(1)}, bf16[192,1024]{1,0:T(8,128)(2,1)S(1)}) %tuple.26, ...), branch_computations={%region_0.0_spmd, %region_1.2_spmd, %region_2.3_spmd, %region_3.4_... | conditional | bytes 5308566 | solution.py:260
  10.8 1.6 %collective-permute-start.3 = (bf16[64,1024]{1,0:T(8,128)(2,1)S(1)}, bf16[64,1024]{1,0:T(8,128)(2,1)S(1)}, u32[]{:S(2)}, u32[]{:S(2)}) collective-permute-start(bf16[64,1024]{1,0:T(8,128)(2,1)S(1)} %slice.21), channel_id=1, source_target_pairs={{0,1},{1,2},{2,3},{3,0},{4,5},{5,6},{6,7},{7,4},{8,9},{9,10},{10,1... | collective-permute-start | bytes 393224 | tf_op jit(solution)/shard_map/cond/branch_2_fun/ppermute | solution.py:28
  12.5 1.1 collective-permute-start.4
  13.6 3.0 %collective-permute-start.5 = (bf16[64,1024]{1,0:T(8,128)(2,1)S(1)}, bf16[64,1024]{1,0:T(8,128)(2,1)S(1)}, u32[]{:S(2)}, u32[]{:S(2)}) collective-permute-start(bf16[64,1024]{1,0:T(8,128)(2,1)S(1)} %slice.23), channel_id=1, source_target_pairs={{0,3},{1,0},{2,1},{3,2},{4,7},{5,4},{6,5},{7,6},{8,11},{9,8},{10,9... | collective-permute-start | bytes 393224 | tf_op jit(solution)/shard_map/cond/branch_2_fun/ppermute | solution.py:28
  16.5 12.9 %collective-permute-done.3 = bf16[64,1024]{1,0:T(8,128)(2,1)S(1)} collective-permute-done((bf16[64,1024]{1,0:T(8,128)(2,1)S(1)}, bf16[64,1024]{1,0:T(8,128)(2,1)S(1)}, u32[]{:S(2)}, u32[]{:S(2)}) %collective-permute-start.3) | collective-permute-done | bytes 131104 | tf_op jit(solution)/shard_map/cond/branch_2_fun/ppermute | solution.py:28
  30.2 3.2 %collective-permute-done.4 = bf16[64,1024]{1,0:T(8,128)(2,1)S(1)} collective-permute-done((bf16[64,1024]{1,0:T(8,128)(2,1)S(1)}, bf16[64,1024]{1,0:T(8,128)(2,1)S(1)}, u32[]{:S(2)}, u32[]{:S(2)}) %collective-permute-start.4) | collective-permute-done | bytes 131104 | tf_op jit(solution)/shard_map/cond/branch_2_fun/ppermute | solution.py:28
  34.2 0.8 pad.26
  35.0 1.5 %collective-permute-start.14 = (bf16[288,1024]{1,0:T(8,128)(2,1)}, bf16[288,1024]{1,0:T(8,128)(2,1)S(1)}, u32[]{:S(2)}, u32[]{:S(2)}) collective-permute-start(bf16[288,1024]{1,0:T(8,128)(2,1)} %get-tuple-element.71), channel_id=1, source_target_pairs={{0,2},{1,3},{2,0},{3,1},{4,6},{5,7},{6,4},{7,5},{8,10},{9,11},{10,... | collective-permute-start | bytes 1769480 | tf_op jit(solution)/shard_map/ppermute | solution.py:28
  36.5 2.1 %collective-permute-start.15 = (bf16[288,1024]{1,0:T(8,128)(2,1)}, bf16[288,1024]{1,0:T(8,128)(2,1)S(1)}, u32[]{:S(2)}, u32[]{:S(2)}) collective-permute-start(bf16[288,1024]{1,0:T(8,128)(2,1)} %get-tuple-element.73), channel_id=1, source_target_pairs={{0,3},{1,0},{2,1},{3,2},{4,7},{5,4},{6,5},{7,6},{8,11},{9,8},{10,9... | collective-permute-start | bytes 1769480 | tf_op jit(solution)/shard_map/ppermute | solution.py:28
  38.6 2.0 %copy-done = bf16[1,448,4096]{2,1,0:T(8,128)(2,1)S(1)} copy-done((bf16[1,448,4096]{2,1,0:T(8,128)(2,1)S(1)}, bf16[1,448,4096]{2,1,0:T(8,128)(2,1)}, u32[]{:S(2)}) %copy-start) | copy-done | bytes 3670040
  40.6 3.6 %shard_map.46 = (bf16[288,1024]{1,0:T(8,128)(2,1)S(1)}, bf16[192,1024]{1,0:T(8,128)(2,1)S(1)}, f32[480,512]{1,0:T(8,128)S(1)}, bf16[1024,512]{1,0:T(8,128)(2,1)S(1)}, f32[1024,512]{1,0:T(8,128)S(1)}) custom-call(s32[2]{0:T(128)S(1)} %copy-done.6, s32[1,28]{1,0:T(1,128)S(1)} %copy-done.5, bf16[448,4096]{1,0:T(8,128)(2,1)S(1)} %bitcast.7, ...), custom_call_target="tpu_custom_call" | custom-call | flops 943718400 | bytes 10485760 | tf_op jit(solution)/shard_map/pallas_call | solution.py:265
  44.2 1.4 copy-done.2
  45.6 17.5 %collective-permute-done.14.refs_2_.refs_8_ = bf16[288,1024]{1,0:T(8,128)(2,1)S(1)} collective-permute-done((bf16[288,1024]{1,0:T(8,128)(2,1)}, bf16[288,1024]{1,0:T(8,128)(2,1)S(1)}, u32[]{:S(2)}, u32[]{:S(2)}) %collective-permute-start.14) | collective-permute-done | bytes 589856 | tf_op jit(solution)/shard_map/ppermute | solution.py:28
  63.1 3.3 %shard_map.48 = (f32[224,512]{1,0:T(8,128)S(1)}, bf16[224,512]{1,0:T(8,128)(2,1)S(1)}, bf16[224,512]{1,0:T(8,128)(2,1)S(1)}, bf16[224,512]{1,0:T(8,128)(2,1)S(1)}) custom-call(s32[2]{0:T(128)S(1)} %copy-done.6, s32[1,28]{1,0:T(1,128)S(1)} %copy-done.5, f32[480,512]{1,0:T(8,128)S(1)} %get-tuple-element.63.keys_ref, ...), custom_call_target="tpu_custom_call" | custom-call | tf_op jit(solution)/shard_map/pallas_call | solution.py:288
  66.4 12.8 %collective-permute-start.16 = (bf16[224,512]{1,0:T(8,128)(2,1)S(1)}, bf16[224,512]{1,0:T(8,128)(2,1)S(1)}, u32[]{:S(2)}, u32[]{:S(2)}) collective-permute-start(bf16[224,512]{1,0:T(8,128)(2,1)S(1)} %get-tuple-element.76), channel_id=1, source_target_pairs={{0,1},{1,2},{2,3},{3,0},{4,5},{5,6},{6,7},{7,4},{8,9},{9,10},{10,1... | collective-permute-start | bytes 688136 | tf_op jit(solution)/shard_map/ppermute | solution.py:28
  79.2 0.8 collective-permute-start.17
  80.0 1.6 %collective-permute-start.18 = (bf16[224,512]{1,0:T(8,128)(2,1)S(1)}, bf16[224,512]{1,0:T(8,128)(2,1)S(1)}, u32[]{:S(2)}, u32[]{:S(2)}) collective-permute-start(bf16[224,512]{1,0:T(8,128)(2,1)S(1)} %get-tuple-element.78), channel_id=1, source_target_pairs={{0,3},{1,0},{2,1},{3,2},{4,7},{5,4},{6,5},{7,6},{8,11},{9,8},{10,9... | collective-permute-start | bytes 688136 | tf_op jit(solution)/shard_map/ppermute | solution.py:28
  81.6 4.4 %collective-permute-done.16 = bf16[224,512]{1,0:T(8,128)(2,1)S(1)} collective-permute-done((bf16[224,512]{1,0:T(8,128)(2,1)S(1)}, bf16[224,512]{1,0:T(8,128)(2,1)S(1)}, u32[]{:S(2)}, u32[]{:S(2)}) %collective-permute-start.16) | collective-permute-done | bytes 229408 | tf_op jit(solution)/shard_map/ppermute | solution.py:28
  86.0 9.2 %collective-permute-done.17 = bf16[224,512]{1,0:T(8,128)(2,1)S(1)} collective-permute-done((bf16[224,512]{1,0:T(8,128)(2,1)S(1)}, bf16[224,512]{1,0:T(8,128)(2,1)S(1)}, u32[]{:S(2)}, u32[]{:S(2)}) %collective-permute-start.17) | collective-permute-done | bytes 229408 | tf_op jit(solution)/shard_map/ppermute | solution.py:28
  95.3 6.6 %collective-permute-start.21 = (bf16[224,512]{1,0:T(8,128)(2,1)S(1)}, bf16[224,512]{1,0:T(8,128)(2,1)S(1)}, u32[]{:S(2)}, u32[]{:S(2)}) collective-permute-start(bf16[224,512]{1,0:T(8,128)(2,1)S(1)} %add_convert_fusion.refs_0_), channel_id=1, source_target_pairs={{0,3},{1,0},{2,1},{3,2},{4,7},{5,4},{6,5},{7,6},{8,11},{9,8},{10,9... | collective-permute-start | bytes 688136 | tf_op jit(solution)/shard_map/ppermute | solution.py:28
  102.5 5.5 %collective-permute-done.21.refs_3_ = bf16[224,512]{1,0:T(8,128)(2,1)S(1)} collective-permute-done((bf16[224,512]{1,0:T(8,128)(2,1)S(1)}, bf16[224,512]{1,0:T(8,128)(2,1)S(1)}, u32[]{:S(2)}, u32[]{:S(2)}) %collective-permute-start.21) | collective-permute-done | bytes 229408 | tf_op jit(solution)/shard_map/ppermute | solution.py:28
  108.0 14.5 %collective-permute-done.20.refs_2_ = bf16[224,512]{1,0:T(8,128)(2,1)S(1)} collective-permute-done((bf16[224,512]{1,0:T(8,128)(2,1)S(1)}, bf16[224,512]{1,0:T(8,128)(2,1)S(1)}, u32[]{:S(2)}, u32[]{:S(2)}) %collective-permute-start.20) | collective-permute-done | bytes 229408 | tf_op jit(solution)/shard_map/ppermute | solution.py:28
  122.5 5.0 %shard_map.49 = (f32[1024,512]{1,0:T(8,128)S(1)}, bf16[1024,512]{1,0:T(8,128)(2,1)S(1)}, f32[8,128]{1,0:T(8,128)S(1)}) custom-call(s32[2]{0:T(128)S(1)} %copy-done.6, s32[1,28]{1,0:T(1,128)S(1)} %copy-done.5, bf16[224,512]{1,0:T(8,128)(2,1)S(1)} %add_convert_fusion.refs_0_, bf16[224,512]{1,0:T(8,128)(2,1)S(1)} %collective-permute-done.19.refs_1_, ...), custom_call_target="tpu_custom_call" | custom-call | tf_op jit(solution)/shard_map/pallas_call | solution.py:306
  127.5 1.3 copy-done.3
  128.9 0.8 collective-permute-start.23
  129.7 2.0 %collective-permute-start.22 = (f32[8,128]{1,0:T(8,128)S(1)}, f32[8,128]{1,0:T(8,128)S(1)}, u32[]{:S(2)}, u32[]{:S(2)}) collective-permute-start(f32[8,128]{1,0:T(8,128)S(1)} %get-tuple-element.81), channel_id=1, source_target_pairs={{0,1},{1,2},{2,3},{3,0},{4,5},{5,6},{6,7},{7,4},{8,9},{9,10},{10,1... | collective-permute-start | bytes 12296 | tf_op jit(solution)/shard_map/ppermute | solution.py:28
  132.5 0.9 collective-permute-done.23
  133.4 1.7 %collective-permute-done.22 = f32[8,128]{1,0:T(8,128)S(1)} collective-permute-done((f32[8,128]{1,0:T(8,128)S(1)}, f32[8,128]{1,0:T(8,128)S(1)}, u32[]{:S(2)}, u32[]{:S(2)}) %collective-permute-start.22) | collective-permute-done | bytes 4128 | tf_op jit(solution)/shard_map/ppermute | solution.py:28
  135.1 1.2 collective-permute-done.25.other_ref
  137.3 4.8 %shard_map.50 = f32[1024,512]{1,0:T(8,128)} custom-call(f32[8,128]{1,0:T(8,128)} %copy-done.8, f32[8,128]{1,0:T(8,128)} %copy-done.9, f32[1024,512]{1,0:T(8,128)} %copy-done.2, f32[1024,512]{1,0:T(8,128)} %copy-done.3, bf16[1024,512]{1,0:T(8,128)(2,1)} %copy-done.7), custom_call_target="tpu_custom_call" | custom-call | tf_op jit(solution)/shard_map/pallas_call | solution.py:328
  (39 shorter events, 5.2 us)
Async XLA Ops:
  0.0 38.5 %collective-permute-start.12 = (f32[1024,512]{1,0:T(8,128)}, f32[1024,512]{1,0:T(8,128)}, u32[]{:S(2)}, u32[]{:S(2)}) collective-permute-start(f32[1024,512]{1,0:T(8,128)} %bitcast.8), channel_id=1, source_target_pairs={{0,4},{4,0},{8,12},{12,8},{16,20},{20,16},{24,28},{28,24},{1,5},{5... | collective-permute-start | bytes 6291464 | tf_op jit(solution)/shard_map/ppermute | solution.py:22
  7.5 38.1 %collective-permute-start.13 = (bf16[288,1024]{1,0:T(8,128)(2,1)}, bf16[288,1024]{1,0:T(8,128)(2,1)S(1)}, u32[]{:S(2)}, u32[]{:S(2)}) collective-permute-start(bf16[288,1024]{1,0:T(8,128)(2,1)} %get-tuple-element.65), channel_id=1, source_target_pairs={{0,1},{1,2},{2,3},{3,0},{4,5},{5,6},{6,7},{7,4},{8,9},{9,10},{10,1... | collective-permute-start | bytes 1769480 | tf_op jit(solution)/shard_map/ppermute | solution.py:28
  10.7 27.8 %copy-start.1 = (f32[1,1024,512]{2,1,0:T(8,128)S(1)}, f32[1,1024,512]{2,1,0:T(8,128)}, u32[]{:S(2)}) copy-start(f32[1,1024,512]{2,1,0:T(8,128)} %param.11) | copy-start | bytes 6291460
  10.7 27.8 %copy-start.4 = (bf16[1,448,512]{2,1,0:T(8,128)(2,1)S(1)}, bf16[1,448,512]{2,1,0:T(8,128)(2,1)}, u32[]{:S(2)}) copy-start(bf16[1,448,512]{2,1,0:T(8,128)(2,1)} %param.10) | copy-start | bytes 1376260
  10.8 27.8 %copy-start.5 = (s32[1,28]{1,0:T(1,128)S(1)}, s32[1,28]{1,0:T(1,128)}, u32[]{:S(2)}) copy-start(s32[1,28]{1,0:T(1,128)} %lengths_ref.7) | copy-start | bytes 340
  10.8 27.8 %copy-start.6 = (s32[2]{0:T(128)S(1)}, s32[2]{0:T(128)}, u32[]{:S(2)}) copy-start(s32[2]{0:T(128)} %pad_add_fusion.index_ref) | copy-start | bytes 28
  10.8 18.6 %collective-permute-start.3 = (bf16[64,1024]{1,0:T(8,128)(2,1)S(1)}, bf16[64,1024]{1,0:T(8,128)(2,1)S(1)}, u32[]{:S(2)}, u32[]{:S(2)}) collective-permute-start(bf16[64,1024]{1,0:T(8,128)(2,1)S(1)} %slice.21), channel_id=1, source_target_pairs={{0,1},{1,2},{2,3},{3,0},{4,5},{5,6},{6,7},{7,4},{8,9},{9,10},{10,1... | collective-permute-start | bytes 393224 | tf_op jit(solution)/shard_map/cond/branch_2_fun/ppermute | solution.py:28
  12.5 21.0 %collective-permute-start.4 = (bf16[64,1024]{1,0:T(8,128)(2,1)S(1)}, bf16[64,1024]{1,0:T(8,128)(2,1)S(1)}, u32[]{:S(2)}, u32[]{:S(2)}) collective-permute-start(bf16[64,1024]{1,0:T(8,128)(2,1)S(1)} %slice.22), channel_id=1, source_target_pairs={{0,2},{1,3},{2,0},{3,1},{4,6},{5,7},{6,4},{7,5},{8,10},{9,11},{10,... | collective-permute-start | bytes 393224 | tf_op jit(solution)/shard_map/cond/branch_2_fun/ppermute | solution.py:28
  13.6 20.6 %collective-permute-start.5 = (bf16[64,1024]{1,0:T(8,128)(2,1)S(1)}, bf16[64,1024]{1,0:T(8,128)(2,1)S(1)}, u32[]{:S(2)}, u32[]{:S(2)}) collective-permute-start(bf16[64,1024]{1,0:T(8,128)(2,1)S(1)} %slice.23), channel_id=1, source_target_pairs={{0,3},{1,0},{2,1},{3,2},{4,7},{5,4},{6,5},{7,6},{8,11},{9,8},{10,9... | collective-permute-start | bytes 393224 | tf_op jit(solution)/shard_map/cond/branch_2_fun/ppermute | solution.py:28
  35.0 28.1 %collective-permute-start.14 = (bf16[288,1024]{1,0:T(8,128)(2,1)}, bf16[288,1024]{1,0:T(8,128)(2,1)S(1)}, u32[]{:S(2)}, u32[]{:S(2)}) collective-permute-start(bf16[288,1024]{1,0:T(8,128)(2,1)} %get-tuple-element.71), channel_id=1, source_target_pairs={{0,2},{1,3},{2,0},{3,1},{4,6},{5,7},{6,4},{7,5},{8,10},{9,11},{10,... | collective-permute-start | bytes 1769480 | tf_op jit(solution)/shard_map/ppermute | solution.py:28
  36.5 26.6 %collective-permute-start.15 = (bf16[288,1024]{1,0:T(8,128)(2,1)}, bf16[288,1024]{1,0:T(8,128)(2,1)S(1)}, u32[]{:S(2)}, u32[]{:S(2)}) collective-permute-start(bf16[288,1024]{1,0:T(8,128)(2,1)} %get-tuple-element.73), channel_id=1, source_target_pairs={{0,3},{1,0},{2,1},{3,2},{4,7},{5,4},{6,5},{7,6},{8,11},{9,8},{10,9... | collective-permute-start | bytes 1769480 | tf_op jit(solution)/shard_map/ppermute | solution.py:28
  38.6 2.0 %copy-start = (bf16[1,448,4096]{2,1,0:T(8,128)(2,1)S(1)}, bf16[1,448,4096]{2,1,0:T(8,128)(2,1)}, u32[]{:S(2)}) copy-start(bf16[1,448,4096]{2,1,0:T(8,128)(2,1)} %param.9) | copy-start | bytes 11010052
  44.2 1.4 copy-start.2
  66.4 19.6 %collective-permute-start.16 = (bf16[224,512]{1,0:T(8,128)(2,1)S(1)}, bf16[224,512]{1,0:T(8,128)(2,1)S(1)}, u32[]{:S(2)}, u32[]{:S(2)}) collective-permute-start(bf16[224,512]{1,0:T(8,128)(2,1)S(1)} %get-tuple-element.76), channel_id=1, source_target_pairs={{0,1},{1,2},{2,3},{3,0},{4,5},{5,6},{6,7},{7,4},{8,9},{9,10},{10,1... | collective-permute-start | bytes 688136 | tf_op jit(solution)/shard_map/ppermute | solution.py:28
  79.2 16.0 %collective-permute-start.17 = (bf16[224,512]{1,0:T(8,128)(2,1)S(1)}, bf16[224,512]{1,0:T(8,128)(2,1)S(1)}, u32[]{:S(2)}, u32[]{:S(2)}) collective-permute-start(bf16[224,512]{1,0:T(8,128)(2,1)S(1)} %get-tuple-element.77), channel_id=1, source_target_pairs={{0,2},{1,3},{2,0},{3,1},{4,6},{5,7},{6,4},{7,5},{8,10},{9,11},{10,... | collective-permute-start | bytes 688136 | tf_op jit(solution)/shard_map/ppermute | solution.py:28
  80.0 15.2 %collective-permute-start.18 = (bf16[224,512]{1,0:T(8,128)(2,1)S(1)}, bf16[224,512]{1,0:T(8,128)(2,1)S(1)}, u32[]{:S(2)}, u32[]{:S(2)}) collective-permute-start(bf16[224,512]{1,0:T(8,128)(2,1)S(1)} %get-tuple-element.78), channel_id=1, source_target_pairs={{0,3},{1,0},{2,1},{3,2},{4,7},{5,4},{6,5},{7,6},{8,11},{9,8},{10,9... | collective-permute-start | bytes 688136 | tf_op jit(solution)/shard_map/ppermute | solution.py:28
  95.3 12.7 %collective-permute-start.21 = (bf16[224,512]{1,0:T(8,128)(2,1)S(1)}, bf16[224,512]{1,0:T(8,128)(2,1)S(1)}, u32[]{:S(2)}, u32[]{:S(2)}) collective-permute-start(bf16[224,512]{1,0:T(8,128)(2,1)S(1)} %add_convert_fusion.refs_0_), channel_id=1, source_target_pairs={{0,3},{1,0},{2,1},{3,2},{4,7},{5,4},{6,5},{7,6},{8,11},{9,8},{10,9... | collective-permute-start | bytes 688136 | tf_op jit(solution)/shard_map/ppermute | solution.py:28
  101.9 20.6 %collective-permute-start.20 = (bf16[224,512]{1,0:T(8,128)(2,1)S(1)}, bf16[224,512]{1,0:T(8,128)(2,1)S(1)}, u32[]{:S(2)}, u32[]{:S(2)}) collective-permute-start(bf16[224,512]{1,0:T(8,128)(2,1)S(1)} %add_convert_fusion.refs_0_), channel_id=1, source_target_pairs={{0,2},{1,3},{2,0},{3,1},{4,6},{5,7},{6,4},{7,5},{8,10},{9,11},{10,... | collective-permute-start | bytes 688136 | tf_op jit(solution)/shard_map/ppermute | solution.py:28
  102.2 20.2 %collective-permute-start.19 = (bf16[224,512]{1,0:T(8,128)(2,1)S(1)}, bf16[224,512]{1,0:T(8,128)(2,1)S(1)}, u32[]{:S(2)}, u32[]{:S(2)}) collective-permute-start(bf16[224,512]{1,0:T(8,128)(2,1)S(1)} %add_convert_fusion.refs_0_), channel_id=1, source_target_pairs={{0,1},{1,2},{2,3},{3,0},{4,5},{5,6},{6,7},{7,4},{8,9},{9,10},{10,1... | collective-permute-start | bytes 688136 | tf_op jit(solution)/shard_map/ppermute | solution.py:28
  127.5 1.3 copy-start.3
  128.8 7.4 %collective-permute-start.26 = (bf16[1024,512]{1,0:T(8,128)(2,1)S(1)}, bf16[1024,512]{1,0:T(8,128)(2,1)S(1)}, u32[]{:S(2)}, u32[]{:S(2)}) collective-permute-start(bf16[1024,512]{1,0:T(8,128)(2,1)S(1)} %get-tuple-element.84), channel_id=1, source_target_pairs={{0,4},{4,0},{8,12},{12,8},{16,20},{20,16},{24,28},{28,24},{1,5},{5... | collective-permute-start | bytes 3145736 | tf_op jit(solution)/shard_map/ppermute | solution.py:22
  128.8 3.6 %collective-permute-start.24 = (f32[8,128]{1,0:T(8,128)S(1)}, f32[8,128]{1,0:T(8,128)S(1)}, u32[]{:S(2)}, u32[]{:S(2)}) collective-permute-start(f32[8,128]{1,0:T(8,128)S(1)} %get-tuple-element.81), channel_id=1, source_target_pairs={{0,3},{1,0},{2,1},{3,2},{4,7},{5,4},{6,5},{7,6},{8,11},{9,8},{10,9... | collective-permute-start | bytes 12296 | tf_op jit(solution)/shard_map/ppermute | solution.py:28
  128.9 4.5 %collective-permute-start.23 = (f32[8,128]{1,0:T(8,128)S(1)}, f32[8,128]{1,0:T(8,128)S(1)}, u32[]{:S(2)}, u32[]{:S(2)}) collective-permute-start(f32[8,128]{1,0:T(8,128)S(1)} %get-tuple-element.81), channel_id=1, source_target_pairs={{0,2},{1,3},{2,0},{3,1},{4,6},{5,7},{6,4},{7,5},{8,10},{9,11},{10,... | collective-permute-start | bytes 12296 | tf_op jit(solution)/shard_map/ppermute | solution.py:28
  129.7 5.4 %collective-permute-start.22 = (f32[8,128]{1,0:T(8,128)S(1)}, f32[8,128]{1,0:T(8,128)S(1)}, u32[]{:S(2)}, u32[]{:S(2)}) collective-permute-start(f32[8,128]{1,0:T(8,128)S(1)} %get-tuple-element.81), channel_id=1, source_target_pairs={{0,1},{1,2},{2,3},{3,0},{4,5},{5,6},{6,7},{7,4},{8,9},{9,10},{10,1... | collective-permute-start | bytes 12296 | tf_op jit(solution)/shard_map/ppermute | solution.py:28
  135.1 1.2 copy-start.8
  135.1 1.2 collective-permute-start.25
  136.3 0.6 copy-start.9
  136.3 1.0 copy-start.7
